TPU v7x, 128 devices: a whole 4x4x4 slice. The times are simulated.
128 devices in a mesh: row: 16 (over z, x), col: 8 (over y, core).
Axes of the slice: x: 4, y: 4, z: 4, core: 2. Of those that a mesh axis runs over, the one named last changes fastest.
Arguments:
- fine_blocks: bfloat16 [64, 32, 64, 576], P('row', 'col'), may hold values from -0.25 to 0.25
- fine_columns: int32 [64, 32, 9], P('row', 'col'), may hold values from 0 to 2047, as said below
- fine_counts: int32 [64, 32], P('row', 'col'), may hold values from 1 to 9, as said below
- prolong_blocks: bfloat16 [64, 32, 64, 256], P('row', 'col'), may hold values from -1.1953125 to 1.1953125
- prolong_columns: int32 [64, 32, 4], P('row', 'col'), may hold values from 0 to 127, as said below
- prolong_counts: int32 [64, 32], P('row', 'col'), may hold values from 1 to 4, as said below
Outputs:
- galerkin: bfloat16 [16, 8, 64, 3136], P('row', 'col')
Inputs may be any that keep to these rules, and one draw needn't show every extreme that they name: `fine_columns`: entry 0 of patch (x, y) is the patch itself; entries 1 to 8 are distinct directions among the eight patches at offsets of at most one along both dimensions, in an order drawn per patch, with coordinates clamped to the grid. `fine_counts`: the patch at the low corner of each 4 x 4 tile uses all 9 blocks. `prolong_columns`: entry 0 of patch (x, y) is its own aggregate (x // 4, y // 4); the other entries are distinct aggregates inside the grid at offsets of at most one from it along both dimensions. `prolong_counts`: the patch at the low corner of each 4 x 4 tile uses all 4 blocks.
All inputs are finite; a program needn't handle non-finite values.
Results may differ from a plain program's by a relative error of at most 0.0049.
Values may be sent and summed in bfloat16 or wider, within the bound.
A program may use at most 128 MiB of HBM per device.

v0:
```python
import functools

import jax
import jax.numpy as jnp
from jax import lax
from jax.experimental import pallas as pl
from jax.experimental.pallas import tpu as pltpu
from jax.sharding import PartitionSpec as P

MESH = pl.DeviceIdType.MESH
F32 = jnp.float32
BF16 = jnp.bfloat16

B = 64
KA = 9
KP = 4
AG = 4
PATCHES = AG * AG
UNUSED = 15
PT_ROWS = KP * B + 16
ORDER = {-1: 0, 1: 1, 0: 2}
WIDE = 26 * B
FULL = 36 * B
R_ROWS = 17 * B


def dot_nn(a, b):
    return lax.dot_general(a, b, (((1,), (0,)), ((), ())), preferred_element_type=F32)


def dot_nt(a, b):
    return lax.dot_general(a, b, (((1,), (1,)), ((), ())), preferred_element_type=F32)


def term_row(down, side):
    return (ORDER[side] * 3 + ORDER[down]) * B


def home(down, side):
    return (side + 1) * 3 + down + 1


def window_row(down, side):
    return (1 + side * 5 + down) * B


def swapped(x):
    return pltpu.roll(x.astype(F32), B, 1)


def slot_parts(x_ref, lanes, width):
    codes = x_ref[KP * B : PT_ROWS, lanes].astype(F32)
    spread = [
        jnp.broadcast_to(codes[p : p + 1], (16, width)).astype(BF16) for p in range(KP)
    ]
    blocks = [x_ref[p * B : (p + 1) * B, lanes].reshape(4, 16, width) for p in range(KP)]
    return spread, blocks


def chosen(spread, blocks, slots, code):
    total = None
    for p in slots:
        part = jnp.where((spread[p] == code)[None], blocks[p], jnp.zeros_like(blocks[p]))
        total = part if total is None else total + part
    return total.reshape(B, total.shape[-1])


def dense(x_ref, lanes, width, places, zeros):
    spread, blocks = slot_parts(x_ref, lanes, width)
    for down in (-1, 0, 1):
        for side in (-1, 0, 1):
            code = home(down, side)
            slots = range(KP) if code == 4 else range(1, KP)
            value = chosen(spread, blocks, slots, jnp.array(code, BF16))
            for ref, row, at in places(down, side):
                ref[row : row + B, at] = value
    for ref, row, at in zeros:
        ref[row : row + B, at] = jnp.zeros((B, width), BF16)


def blank_rows(ref, at, downs):
    rows = [0, 16 * B] + [window_row(d, s) for s in range(3) for d in downs]
    return [(ref, row, at) for row in rows]


def kernel(
    p_hbm, a_hbm, acode_ref, pcode_ref, out_ref,
    pv, av, ptx, edge_l, edge_r, halo_t, halo_b, halo_l, halo_r,
    pass_l, pass_r, corner_l, corner_r,
    pdt, aw, q_own, q_l, q_r, r_own, r_l, r_r, c_side, c_mid,
    send_l, send_r, got_l, got_r, send_rows, e_mid, got_u, got_d,
    in_sem, send_sem, recv_sem,
):
    row, col = lax.axis_index("row"), lax.axis_index("col")
    rows, cols = lax.axis_size("row"), lax.axis_size("col")
    up = {"row": lax.rem(row + rows - 1, rows)}
    down = {"row": lax.rem(row + 1, rows)}
    left = {"col": lax.rem(col + cols - 1, cols)}
    right = {"col": lax.rem(col + 1, cols)}

    p_in = pltpu.make_async_copy(p_hbm, pv, in_sem.at[0])
    a_in = pltpu.make_async_copy(a_hbm, av, in_sem.at[1])
    p_in.start()
    a_in.start()
    barrier = pltpu.get_barrier_semaphore()
    for peer in (up, down, left, right):
        pl.semaphore_signal(barrier, inc=1, device_id=peer, device_id_type=MESH)

    def remote(number, src, dst, peer):
        return pltpu.make_async_remote_copy(
            src_ref=src,
            dst_ref=dst,
            send_sem=send_sem.at[number],
            recv_sem=recv_sem.at[number],
            device_id=peer,
            device_id_type=MESH,
        )

    eye = (
        lax.broadcasted_iota(jnp.int32, (256, 256), 0)
        == lax.broadcasted_iota(jnp.int32, (256, 256), 1)
    ).astype(F32).astype(BF16)
    p_in.wait()
    for side, edge in ((0, edge_l), (AG - 1, edge_r)):
        edge[0 : KP * B, :] = dot_nt(eye, pv[:, side].reshape(256, 256)).astype(BF16)
    edge_l[KP * B :, :] = pcode_ref[:, 1024:1280]
    edge_r[KP * B :, :] = pcode_ref[:, 1280:1536]
    for u in range(AG):
        ptx[0 : KP * B, u * 256 : (u + 1) * 256] = dot_nt(
            eye, pv[u].reshape(256, 256)
        ).astype(BF16)
    ptx[KP * B :, :] = pcode_ref[:, 0:1024]

    pl.semaphore_wait(barrier, 4)
    to_up = remote(0, ptx.at[:, 0:256], halo_b, up)
    to_down = remote(1, ptx.at[:, 768:1024], halo_t, down)
    to_left = remote(2, edge_l, halo_r, left)
    to_right = remote(3, edge_r, halo_l, right)
    for copy in (to_up, to_down, to_left, to_right):
        copy.start()

    def own_dense(u, carry):
        lanes = pl.ds(pl.multiple_of(u * 256, 256), 256)
        dense(
            ptx, lanes, 256,
            lambda d, s: [
                (pdt, term_row(d, s), lanes),
                (r_own, window_row(d + 2, s + 1), lanes),
            ],
            blank_rows(r_own, lanes, (0, 4)),
        )
        return carry

    lax.fori_loop(0, AG, own_dense, 0)

    a_in.wait()
    lane = lax.broadcasted_iota(jnp.int32, (1, 128), 1)
    tiles = ((1, 2), (3, 4), (0, 5))

    def strip(u, carry):
        for v in range(AG):
            wide = [av[u, v, :, 128 * t : 128 * (t + 1)] for t in range(4)]
            last = av[u, v, :, 512:576]
            wide.append(jnp.concatenate([last, jnp.zeros_like(last)], axis=1))
            wide = wide + [swapped(w).astype(BF16) for w in wide]
            wide = [w.reshape(4, 16, 128) for w in wide]
            codes = acode_ref[u * AG + v]
            for at, pair in enumerate(tiles):
                sides = [target - 1 - v for target in pair]
                for dr in (-1, 0, 1):
                    here = (u + dr + 1, pl.ds((1 - dr) * 256 + v * B, B), pl.ds(at * 128, 128))
                    wanted = [(dr + 1) * 3 + dc + 1 if abs(dc) <= 1 else 99 for dc in sides]
                    if wanted == [99, 99]:
                        aw[here] = jnp.zeros((B, 128), BF16)
                        continue
                    match = jnp.where(
                        codes == jnp.where(lane < B, wanted[0], wanted[1]).astype(F32), 1.0, 0.0
                    )
                    total = None
                    for t in range(10):
                        if wanted[0] == 99 and t == 4 or wanted[1] == 99 and t == 9:
                            continue
                        mask = jnp.broadcast_to(match[t : t + 1], (16, 128)).astype(BF16)
                        part = mask[None] * wide[t]
                        total = part if total is None else total + part
                    aw[here] = total.reshape(B, 128)
        return carry

    lax.fori_loop(0, AG, strip, 0)

    def row_of_targets(w):
        first, last = max(w - 1, 0), min(w + 1, AG - 1)
        got = dot_nn(
            pdt[:, first * 256 : (last + 1) * 256],
            aw[w + 1, (first - w + 1) * 256 : (last - w + 2) * 256, :],
        )
        place = w if 0 <= w < AG else (AG if w < 0 else AG + 1)
        q_own[:, place * 256 : (place + 1) * 256] = got[:, 0:256].astype(BF16)
        return got[:, 256:384]

    half = lane < B
    for at, (w0, w1) in enumerate(((0, 1), (2, 3), (-1, 4))):
        x, y = row_of_targets(w0), row_of_targets(w1)
        lanes = slice(at * 128, (at + 1) * 128)
        q_l[:, lanes] = jnp.where(half, x, pltpu.roll(y, B, 1)).astype(BF16)
        q_r[:, lanes] = jnp.where(half, pltpu.roll(x, B, 1), y).astype(BF16)

    c_side[:, 0:256] = jnp.zeros((384, 256), F32)
    c_side[:, 1280:WIDE] = jnp.zeros((384, WIDE - 1280), F32)
    c_mid[:, 0:384] = jnp.zeros((192, 384), F32)
    c_mid[:, 1408:WIDE] = jnp.zeros((192, WIDE - 1408), F32)
    c_side[:, 256:1280] = dot_nt(q_own[0:384, 0:1024], r_own[0:1024, 0:1024])
    c_mid[:, 384:1408] = dot_nt(q_own[384:576, 0:1024], r_own[64:1088, 0:1024])

    to_down.wait_recv()
    to_up.wait_recv()
    for rows_16 in range(PT_ROWS // 16):
        at = slice(rows_16 * 16, (rows_16 + 1) * 16)
        pass_l[at, :] = jnp.where(
            half, halo_t[at, 0:128].astype(F32), swapped(halo_b[at, 0:128])
        ).astype(BF16)
        pass_r[at, :] = jnp.where(
            half, swapped(halo_t[at, 128:256]), halo_b[at, 128:256].astype(F32)
        ).astype(BF16)
    corner_to_left = remote(4, pass_l, corner_r, left)
    corner_to_right = remote(5, pass_r, corner_l, right)
    corner_to_left.start()
    corner_to_right.start()

    for halo, shift, blanks, first in ((halo_t, 1, (3, 4), 1024), (halo_b, 3, (0, 1), 1280)):
        at = slice(first, first + 256)
        dense(
            halo, slice(0, 256), 256,
            lambda d, s: [(r_own, window_row(d + shift, s + 1), at)],
            blank_rows(r_own, at, blanks),
        )
    to_left.wait_recv()
    to_right.wait_recv()
    for halo, ref in ((halo_l, r_l), (halo_r, r_r)):
        at = slice(0, 256)
        dense(
            halo, at, 256,
            lambda d, s: [(ref, window_row(d + 2, s + 1), at)],
            blank_rows(ref, at, (0, 4)),
        )
    c_side[:, 256:1280] += dot_nt(q_own[0:384, 1024:1536], r_own[0:1024, 1024:1536])

    corner_to_left.wait_recv()
    corner_to_right.wait_recv()
    for corner, ref in ((corner_l, r_l), (corner_r, r_r)):
        spread, blocks = slot_parts(corner, slice(0, 128), 128)
        for side in (-1, 0, 1):
            for j in range(5):
                above, below = j - 1, j - 3
                codes = [home(d, side) if abs(d) <= 1 else 99 for d in (above, below)]
                code = jnp.where(half, codes[0], codes[1]).astype(F32).astype(BF16)
                row_at = window_row(j, side + 1)
                ref[row_at : row_at + B, 256:384] = chosen(spread, blocks, range(KP), code)
        for row_at in (0, 16 * B):
            ref[row_at : row_at + B, 256:384] = jnp.zeros((B, 128), BF16)
    c_side[:, 0:1024] += dot_nt(q_l[0:384, :], r_l[64:1088, :])
    c_side[:, 640:WIDE] += dot_nt(q_r[0:384, :], r_r[64:1088, :])

    send_l[...] = c_side[0:192, :].astype(BF16)
    send_r[...] = c_side[192:384, :].astype(BF16)
    side_copies = []
    for number, at in ((6, slice(0, 128)), (8, slice(128, 192))):
        to_l = remote(number, send_l.at[at], got_r.at[at], left)
        to_r = remote(number + 1, send_r.at[at], got_l.at[at], right)
        to_l.start()
        to_r.start()
        side_copies.append((to_l, to_r))

    c_mid[:, 384:1408] += dot_nt(q_own[384:576, 1024:1536], r_own[64:1088, 1024:1536])
    c_mid[:, 0:1024] += dot_nt(q_l[384:576, :], r_l[0:1024, :])
    c_mid[:, 640:WIDE] += dot_nt(q_r[384:576, :], r_r[0:1024, :])

    def folded(at, lo, hi):
        total = None
        for ref, first in ((got_l, 0), (c_mid, 256), (got_r, 640)):
            if first <= lo and hi <= first + WIDE:
                part = ref[at, lo - first : hi - first].astype(F32)
                total = part if total is None else total + part
        return total

    spans = ((0, 256), (256, 640), (640, 1664), (1664, 1920), (1920, FULL))
    for copy in side_copies[0]:
        copy.wait_recv()
    for lo, hi in spans:
        send_rows[:, lo:hi] = folded(slice(0, 128), lo, hi).astype(BF16)
    to_u = remote(10, send_rows.at[0:64], got_d, up)
    to_d = remote(11, send_rows.at[64:128], got_u, down)
    to_u.start()
    to_d.start()
    for copy in side_copies[1]:
        copy.wait_recv()
    for lo, hi in spans:
        e_mid[:, lo:hi] = folded(slice(128, 192), lo, hi)
    to_u.wait_recv()
    to_d.wait_recv()

    for s in range(7):
        for t in range(7):
            total = None
            for ref, j in ((got_u, s), (e_mid, s - 1), (got_d, s - 2)):
                if 0 <= j < 5:
                    at = (t * 5 + j) * B
                    part = ref[:, at : at + B].astype(F32)
                    total = part if total is None else total + part
            at = (s * 7 + t) * B
            out_ref[0, 0, :, at : at + B] = total.astype(BF16)

    sent = [to_up, to_down, to_left, to_right, corner_to_left, corner_to_right, to_u, to_d]
    for copy in sent + [copy for pair in side_copies for copy in pair]:
        copy.wait_send()


def slot_codes(fine_columns, fine_counts, prolong_columns, prolong_counts):
    row, col = lax.axis_index("row"), lax.axis_index("col")
    fine_cols = AG * lax.axis_size("col")
    coarse_cols = lax.axis_size("col")
    steps = jnp.arange(AG, dtype=jnp.int32)
    patch_row = (row * AG + steps)[:, None, None]
    patch_col = (col * AG + steps)[None, :, None]
    toward = (fine_columns // fine_cols - patch_row + 1) * 3 + fine_columns % fine_cols - patch_col + 1
    used = jnp.arange(KA, dtype=jnp.int32) < fine_counts[:, :, None]
    toward = jnp.where(used, toward, UNUSED).astype(F32).reshape(PATCHES, KA)
    toward = jnp.pad(toward, ((0, 0), (0, 1)), constant_values=UNUSED).reshape(PATCHES, 5, 2)
    both = jnp.concatenate([toward, toward[:, :, ::-1]], axis=1)
    acode = jnp.broadcast_to(both[..., None], (PATCHES, 10, 2, B)).reshape(PATCHES, 10, 2 * B)

    home_slot = (prolong_columns % coarse_cols - col + 1) * 3 + prolong_columns // coarse_cols - row + 1
    used = jnp.arange(KP, dtype=jnp.int32) < prolong_counts[:, :, None]
    home_slot = jnp.where(used, home_slot, UNUSED).astype(BF16).transpose(2, 0, 1)
    order = [home_slot.reshape(KP, PATCHES), home_slot[:, :, 0], home_slot[:, :, AG - 1]]
    order = jnp.pad(jnp.concatenate(order, axis=1), ((0, 16 - KP), (0, 0)))
    pcode = jnp.broadcast_to(order[:, :, None], (16, 24, B)).reshape(16, 24 * B)
    return acode, pcode


def per_device(
    fine_blocks, fine_columns, fine_counts, prolong_blocks, prolong_columns, prolong_counts
):
    acode, pcode = slot_codes(fine_columns, fine_counts, prolong_columns, prolong_counts)
    vmem = pl.BlockSpec(memory_space=pltpu.VMEM)
    hbm = pl.BlockSpec(memory_space=pl.ANY)
    return pl.pallas_call(
        kernel,
        out_shape=jax.ShapeDtypeStruct((1, 1, B, 49 * B), BF16),
        in_specs=[hbm, hbm, vmem, vmem],
        out_specs=vmem,
        scratch_shapes=[
            pltpu.VMEM((AG, AG, B, KP * B), BF16),
            pltpu.VMEM((AG, AG, B, KA * B), BF16),
            pltpu.VMEM((PT_ROWS, 1024), BF16),
            pltpu.VMEM((PT_ROWS, 256), BF16),
            pltpu.VMEM((PT_ROWS, 256), BF16),
            pltpu.VMEM((PT_ROWS, 256), BF16),
            pltpu.VMEM((PT_ROWS, 256), BF16),
            pltpu.VMEM((PT_ROWS, 256), BF16),
            pltpu.VMEM((PT_ROWS, 256), BF16),
            pltpu.VMEM((PT_ROWS, 128), BF16),
            pltpu.VMEM((PT_ROWS, 128), BF16),
            pltpu.VMEM((PT_ROWS, 128), BF16),
            pltpu.VMEM((PT_ROWS, 128), BF16),
            pltpu.VMEM((9 * B, 1024), BF16),
            pltpu.VMEM((6, 768, 384), BF16),
            pltpu.VMEM((9 * B, 1536), BF16),
            pltpu.VMEM((9 * B, 384), BF16),
            pltpu.VMEM((9 * B, 384), BF16),
            pltpu.VMEM((R_ROWS, 1536), BF16),
            pltpu.VMEM((R_ROWS, 384), BF16),
            pltpu.VMEM((R_ROWS, 384), BF16),
            pltpu.VMEM((6 * B, WIDE), F32),
            pltpu.VMEM((3 * B, WIDE), F32),
            pltpu.VMEM((3 * B, WIDE), BF16),
            pltpu.VMEM((3 * B, WIDE), BF16),
            pltpu.VMEM((3 * B, WIDE), BF16),
            pltpu.VMEM((3 * B, WIDE), BF16),
            pltpu.VMEM((2 * B, FULL), BF16),
            pltpu.VMEM((B, FULL), F32),
            pltpu.VMEM((B, FULL), BF16),
            pltpu.VMEM((B, FULL), BF16),
            pltpu.SemaphoreType.DMA((2,)),
            pltpu.SemaphoreType.DMA((12,)),
            pltpu.SemaphoreType.DMA((12,)),
        ],
        compiler_params=pltpu.CompilerParams(
            collective_id=0, has_side_effects=True, vmem_limit_bytes=48 * 2**20
        ),
    )(prolong_blocks, fine_blocks, acode, pcode)


def solution(mesh):
    in_specs = (
        P("row", "col", None, None),
        P("row", "col", None),
        P("row", "col"),
        P("row", "col", None, None),
        P("row", "col", None),
        P("row", "col"),
    )
    return jax.shard_map(
        per_device,
        mesh=mesh,
        in_specs=in_specs,
        out_specs=P("row", "col", None, None),
        check_vma=False,
    )
```

profile of v0, /device:TPU:24, one launch (start us, length us, event | category | flops | bytes accessed | tf_op | source)
XLA Modules:
  0.0 40.0 jit_solution(3752486930081926723)
XLA Ops:
  0.0 0.0 copy-start.1
  0.0 0.8 %fusion.23 = bf16[4,4,4]{0,2,1:T(4,128)(2,1)S(1)} fusion(s32[]{:T(128)S(6)} %axis_index.23, s32[4,4,4]{2,1,0:T(4,128)} %param.10, s32[]{:T(128)S(6)} %axis_index.25, s32[4,4]{1,0:T(4,128)} %param.11), kind=kLoop, calls=%fused_computation.42 | loop fusion | flops 1792 | bytes 456 | tf_op jit(solution)/shard_map/transpose | solution.py:334
  0.8 0.1 copy.13
  1.0 0.1 copy.14
  1.1 0.8 %fusion.18 = bf16[4,4,4]{2,1,0:T(4,128)(2,1)S(1)} fusion(s32[4,4,4]{2,1,0:T(4,128)} %param.10, s32[]{:T(128)S(6)} %axis_index.23, s32[]{:T(128)S(6)} %axis_index.25, s32[4,4]{1,0:T(4,128)} %param.11), kind=kLoop, calls=%fused_computation.35 | loop fusion | flops 1792 | bytes 456 | tf_op jit(solution)/shard_map/convert_element_type | solution.py:334
  1.8 0.1 copy.16
  1.9 0.1 fusion.21
  2.0 0.8 %select_convert_fusion = f32[4,4,9]{2,1,0:T(4,128)S(1)} fusion(s32[4,4,9]{2,1,0:T(4,128)} %param.7, s32[4]{0:T(128)S(1)} %get-tuple-element.7, s32[4]{0:T(128)S(1)} %get-tuple-element.8, s32[4,4]{1,0:T(4,128)} %param.8), kind=kLoop, calls=%fused_computation.29 | loop fusion | flops 4032 | bytes 1248 | tf_op jit(solution)/shard_map/convert_element_type | solution.py:327
  2.8 0.1 copy.10
  2.9 0.1 copy.11
  3.1 0.2 broadcast_in_dim.12
  3.3 0.1 reshape.29
  3.5 0.1 broadcast_in_dim.15
  3.6 0.1 reshape.31.pcode_ref
  3.7 0.0 copy-done.1
  3.8 0.0 copy-start
  3.8 1.3 %copy-done = bf16[4,4,64,576]{3,2,1,0:T(8,128)(2,1)S(1)} copy-done((bf16[4,4,64,576]{3,2,1,0:T(8,128)(2,1)S(1)}, bf16[4,4,64,576]{3,2,1,0:T(8,128)(2,1)}, u32[]{:S(2)}) %copy-start) | copy-done | bytes 1179672
  5.1 34.2 %shard_map.64 = bf16[1,1,64,3136]{3,2,1,0:T(8,128)(2,1)S(1)} custom-call(bf16[4,4,64,256]{3,2,1,0:T(8,128)(2,1)S(1)} %copy-done.1, bf16[4,4,64,576]{3,2,1,0:T(8,128)(2,1)S(1)} %copy-done, f32[16,10,128]{2,1,0:T(8,128)S(1)} %copy.15.acode_ref, bf16[16,1536]{1,0:T(8,128)(2,1)S(1)} %reshape.31.pcode_ref), custom_call_target="tpu_custom_call" | custom-call | tf_op jit(solution)/shard_map/pallas_call | solution.py:347
  39.3 0.8 %copy.18 = bf16[1,1,64,3136]{3,2,1,0:T(8,128)(2,1)} copy(bf16[1,1,64,3136]{3,2,1,0:T(8,128)(2,1)S(1)} %shard_map.64) | data formatting | bytes 802816
  (7 shorter events, 0.1 us)
Async XLA Ops:
  0.0 3.7 %copy-start.1 = (bf16[4,4,64,256]{3,2,1,0:T(8,128)(2,1)S(1)}, bf16[4,4,64,256]{3,2,1,0:T(8,128)(2,1)}, u32[]{:S(2)}) copy-start(bf16[4,4,64,256]{3,2,1,0:T(8,128)(2,1)} %p_hbm.1) | copy-start | bytes 1572868
  3.8 1.3 %copy-start = (bf16[4,4,64,576]{3,2,1,0:T(8,128)(2,1)S(1)}, bf16[4,4,64,576]{3,2,1,0:T(8,128)(2,1)}, u32[]{:S(2)}) copy-start(bf16[4,4,64,576]{3,2,1,0:T(8,128)(2,1)} %a_hbm.1) | copy-start | bytes 3538948
where the time goes:
time: 40.3 us; the launch traced here: 40 us
  Pallas kernels  34.2 us (85%)
  local copies, waits for them, and re-layouts  3.3 us (8%)
  other arithmetic  2.48 us (6%)
    pallas_call x1, Pallas kernels, per_device(): pl.pallas_call(kernel, out_shape=jax.ShapeDtypeStruct((1, 1, B, 49 * B),...  34.2 us
    unnamed x5, local copies, waits for them, and re-layouts  2.07 us
    transpose x1, other arithmetic, slot_codes(): jnp.where(used, home_slot, UNUSED).astype(BF16).transpose(2, 0, 1)  0.83 us

commit v1 on v0

--- a/solution.py
+++ b/solution.py
@@ -15,7 +15,6 @@
 KA = 9
 KP = 4
 AG = 4
-PATCHES = AG * AG
 UNUSED = 15
 PT_ROWS = KP * B + 16
 ORDER = {-1: 0, 1: 1, 0: 2}
@@ -84,7 +83,7 @@
 
 
 def kernel(
-    p_hbm, a_hbm, acode_ref, pcode_ref, out_ref,
+    p_hbm, a_hbm, fine_columns, fine_counts, prolong_columns, prolong_counts, out_ref,
     pv, av, ptx, edge_l, edge_r, halo_t, halo_b, halo_l, halo_r,
     pass_l, pass_r, corner_l, corner_r,
     pdt, aw, q_own, q_l, q_r, r_own, r_l, r_r, c_side, c_mid,
@@ -93,6 +92,7 @@
 ):
     row, col = lax.axis_index("row"), lax.axis_index("col")
     rows, cols = lax.axis_size("row"), lax.axis_size("col")
+    fine_cols = AG * cols
     up = {"row": lax.rem(row + rows - 1, rows)}
     down = {"row": lax.rem(row + 1, rows)}
     left = {"col": lax.rem(col + cols - 1, cols)}
@@ -120,16 +120,37 @@
         lax.broadcasted_iota(jnp.int32, (256, 256), 0)
         == lax.broadcasted_iota(jnp.int32, (256, 256), 1)
     ).astype(F32).astype(BF16)
+    lane = lax.broadcasted_iota(jnp.int32, (1, 128), 1)
+    line = lax.broadcasted_iota(jnp.int32, (16, 128), 0)
+    half = lane < B
+
+    def home_code(u, v, p):
+        number = prolong_columns[u, v, p]
+        code = (lax.bitwise_and(number, cols - 1) - col + 1) * 3 - row + 1
+        code += lax.shift_right_logical(number, cols.bit_length() - 1)
+        return jnp.where(p < prolong_counts[u, v], code, UNUSED)
+
+    codes = {(u, v): [home_code(u, v, p) for p in range(KP)] for u in range(AG) for v in range(AG)}
+
+    def code_tile(ref, at, first, second):
+        tile = jnp.zeros((16, 128), jnp.int32)
+        for p in range(KP):
+            tile = jnp.where(line == p, jnp.where(half, codes[first][p], codes[second][p]), tile)
+        ref[KP * B :, at * 128 : (at + 1) * 128] = tile.astype(F32).astype(BF16)
+
+    for u in range(AG):
+        code_tile(ptx, 2 * u, (u, 0), (u, 1))
+        code_tile(ptx, 2 * u + 1, (u, 2), (u, 3))
+    for side, edge in ((0, edge_l), (AG - 1, edge_r)):
+        code_tile(edge, 0, (0, side), (1, side))
+        code_tile(edge, 1, (2, side), (3, side))
     p_in.wait()
     for side, edge in ((0, edge_l), (AG - 1, edge_r)):
         edge[0 : KP * B, :] = dot_nt(eye, pv[:, side].reshape(256, 256)).astype(BF16)
-    edge_l[KP * B :, :] = pcode_ref[:, 1024:1280]
-    edge_r[KP * B :, :] = pcode_ref[:, 1280:1536]
     for u in range(AG):
         ptx[0 : KP * B, u * 256 : (u + 1) * 256] = dot_nt(
             eye, pv[u].reshape(256, 256)
         ).astype(BF16)
-    ptx[KP * B :, :] = pcode_ref[:, 0:1024]
 
     pl.semaphore_wait(barrier, 4)
     to_up = remote(0, ptx.at[:, 0:256], halo_b, up)
@@ -154,8 +175,13 @@
     lax.fori_loop(0, AG, own_dense, 0)
 
     a_in.wait()
-    lane = lax.broadcasted_iota(jnp.int32, (1, 128), 1)
     tiles = ((1, 2), (3, 4), (0, 5))
+
+    def toward_code(u, v, k):
+        number = fine_columns[u, v, k]
+        code = (lax.shift_right_logical(number, fine_cols.bit_length() - 1) - row * AG - u) * 3
+        code += lax.bitwise_and(number, fine_cols - 1) - col * AG - v + 4
+        return jnp.where(k < fine_counts[u, v], code, UNUSED)
 
     def strip(u, carry):
         for v in range(AG):
@@ -164,7 +190,12 @@
             wide.append(jnp.concatenate([last, jnp.zeros_like(last)], axis=1))
             wide = wide + [swapped(w).astype(BF16) for w in wide]
             wide = [w.reshape(4, 16, 128) for w in wide]
-            codes = acode_ref[u * AG + v]
+            codes = jnp.full((16, 128), UNUSED, jnp.int32)
+            toward = [toward_code(u, v, k) for k in range(KA)] + [UNUSED]
+            for t in range(5):
+                one, two = toward[2 * t], toward[2 * t + 1]
+                codes = jnp.where(line == t, jnp.where(half, one, two), codes)
+                codes = jnp.where(line == t + 5, jnp.where(half, two, one), codes)
             for at, pair in enumerate(tiles):
                 sides = [target - 1 - v for target in pair]
                 for dr in (-1, 0, 1):
@@ -174,7 +205,7 @@
                         aw[here] = jnp.zeros((B, 128), BF16)
                         continue
                     match = jnp.where(
-                        codes == jnp.where(lane < B, wanted[0], wanted[1]).astype(F32), 1.0, 0.0
+                        codes == jnp.where(half, wanted[0], wanted[1]), 1.0, 0.0
                     )
                     total = None
                     for t in range(10):
@@ -198,7 +229,6 @@
         q_own[:, place * 256 : (place + 1) * 256] = got[:, 0:256].astype(BF16)
         return got[:, 256:384]
 
-    half = lane < B
     for at, (w0, w1) in enumerate(((0, 1), (2, 3), (-1, 4))):
         x, y = row_of_targets(w0), row_of_targets(w1)
         lanes = slice(at * 128, (at + 1) * 128)
@@ -315,39 +345,16 @@
         copy.wait_send()
 
 
-def slot_codes(fine_columns, fine_counts, prolong_columns, prolong_counts):
-    row, col = lax.axis_index("row"), lax.axis_index("col")
-    fine_cols = AG * lax.axis_size("col")
-    coarse_cols = lax.axis_size("col")
-    steps = jnp.arange(AG, dtype=jnp.int32)
-    patch_row = (row * AG + steps)[:, None, None]
-    patch_col = (col * AG + steps)[None, :, None]
-    toward = (fine_columns // fine_cols - patch_row + 1) * 3 + fine_columns % fine_cols - patch_col + 1
-    used = jnp.arange(KA, dtype=jnp.int32) < fine_counts[:, :, None]
-    toward = jnp.where(used, toward, UNUSED).astype(F32).reshape(PATCHES, KA)
-    toward = jnp.pad(toward, ((0, 0), (0, 1)), constant_values=UNUSED).reshape(PATCHES, 5, 2)
-    both = jnp.concatenate([toward, toward[:, :, ::-1]], axis=1)
-    acode = jnp.broadcast_to(both[..., None], (PATCHES, 10, 2, B)).reshape(PATCHES, 10, 2 * B)
-
-    home_slot = (prolong_columns % coarse_cols - col + 1) * 3 + prolong_columns // coarse_cols - row + 1
-    used = jnp.arange(KP, dtype=jnp.int32) < prolong_counts[:, :, None]
-    home_slot = jnp.where(used, home_slot, UNUSED).astype(BF16).transpose(2, 0, 1)
-    order = [home_slot.reshape(KP, PATCHES), home_slot[:, :, 0], home_slot[:, :, AG - 1]]
-    order = jnp.pad(jnp.concatenate(order, axis=1), ((0, 16 - KP), (0, 0)))
-    pcode = jnp.broadcast_to(order[:, :, None], (16, 24, B)).reshape(16, 24 * B)
-    return acode, pcode
-
-
 def per_device(
     fine_blocks, fine_columns, fine_counts, prolong_blocks, prolong_columns, prolong_counts
 ):
-    acode, pcode = slot_codes(fine_columns, fine_counts, prolong_columns, prolong_counts)
     vmem = pl.BlockSpec(memory_space=pltpu.VMEM)
+    smem = pl.BlockSpec(memory_space=pltpu.SMEM)
     hbm = pl.BlockSpec(memory_space=pl.ANY)
     return pl.pallas_call(
         kernel,
         out_shape=jax.ShapeDtypeStruct((1, 1, B, 49 * B), BF16),
-        in_specs=[hbm, hbm, vmem, vmem],
+        in_specs=[hbm, hbm, smem, smem, smem, smem],
         out_specs=vmem,
         scratch_shapes=[
             pltpu.VMEM((AG, AG, B, KP * B), BF16),
@@ -386,9 +393,12 @@
             pltpu.SemaphoreType.DMA((12,)),
         ],
         compiler_params=pltpu.CompilerParams(
-            collective_id=0, has_side_effects=True, vmem_limit_bytes=48 * 2**20
+            collective_id=0, has_side_effects=True, vmem_limit_bytes=60 * 2**20
         ),
-    )(prolong_blocks, fine_blocks, acode, pcode)
+    )(
+        prolong_blocks, fine_blocks,
+        fine_columns, fine_counts, prolong_columns, prolong_counts,
+    )
 
 
 def solution(mesh):

time: 40.3 us -> 37.8 us (0.938)
  other arithmetic: 2.48 us -> 0 us
  Pallas kernels: 34.2 us -> 35.8 us
  local copies, waits for them, and re-layouts: 3.3 us -> 1.78 us
    pallas_call x1, Pallas kernels: 34.2 us -> 35.8 us  [per_device(): pl.pallas_call(kernel, out_shape=jax.ShapeDtypeStruct((1, 1, B, 49 * B),...]
    convert_element_type x2 -> x0, other arithmetic: 1.55 us -> none  [the longest x1 0.78 us: slot_codes(): toward = jnp.where(used, toward, UNUSED).astype(F32).reshape(PATCHES, KA)]
    transpose x1 -> x0, other arithmetic: 0.83 us -> none  [slot_codes(): jnp.where(used, home_slot, UNUSED).astype(BF16).transpose(2, 0, 1)]
    reshape x6 -> x0, local copies, waits for them, and re-layouts: 0.49 us -> none  [the longest x2 0.17 us: slot_codes(): jnp.broadcast_to(both[..., None], (PATCHES, 10, 2, B))]
    unnamed x5 -> x1, local copies, waits for them, and re-layouts: 2.07 us -> 1.78 us
where the time goes in v1:
time: 37.8 us; the launch traced here: 37.6 us
  Pallas kernels  35.8 us (95%)
  local copies, waits for them, and re-layouts  1.78 us (5%)
    pallas_call x1, Pallas kernels, per_device(): pl.pallas_call(kernel, out_shape=jax.ShapeDtypeStruct((1, 1, B, 49 * B),...  35.8 us
    unnamed x1, local copies, waits for them, and re-layouts  1.78 us

profile of v1, /device:TPU:24, one launch (start us, length us, event | category | flops | bytes accessed | tf_op | source)
XLA Modules:
  0.0 37.6 jit_solution(1075354268694413)
XLA Ops:
  0.0 35.8 %shard_map.64 = bf16[1,1,64,3136]{3,2,1,0:T(8,128)(2,1)} custom-call(bf16[4,4,64,256]{3,2,1,0:T(8,128)(2,1)} %p_hbm.1, bf16[4,4,64,576]{3,2,1,0:T(8,128)(2,1)} %a_hbm.1, s32[4,4,9]{2,1,0:T(4,128)} %fine_columns.1, s32[4,4]{1,0:T(4,128)} %fine_counts.1, s32[4,4,4]{2,1,0:T(4,128)} %prolong_columns.1, s32[4,4]{1,0:T(4,128)} %prolong_counts.1), custom_call_target="tpu_custom_call" | custom-call | tf_op jit(solution)/shard_map/pallas_call | solution.py:354
  35.8 1.8 %copy.8 = bf16[1,1,64,3136]{3,2,1,0:T(8,128)(2,1)} copy(bf16[1,1,64,3136]{3,2,1,0:T(8,128)(2,1)} %shard_map.64) | data formatting | bytes 802816

commit v2 on v1

--- a/solution.py
+++ b/solution.py
@@ -83,7 +83,8 @@
 
 
 def kernel(
-    p_hbm, a_hbm, fine_columns, fine_counts, prolong_columns, prolong_counts, out_ref,
+    p_hbm, a_hbm, fine_columns_hbm, fine_counts_hbm, prolong_columns_hbm, prolong_counts_hbm, out_ref,
+    fine_columns, fine_counts, prolong_columns, prolong_counts,
     pv, av, ptx, edge_l, edge_r, halo_t, halo_b, halo_l, halo_r,
     pass_l, pass_r, corner_l, corner_r,
     pdt, aw, q_own, q_l, q_r, r_own, r_l, r_r, c_side, c_mid,
@@ -93,28 +94,63 @@
     row, col = lax.axis_index("row"), lax.axis_index("col")
     rows, cols = lax.axis_size("row"), lax.axis_size("col")
     fine_cols = AG * cols
-    up = {"row": lax.rem(row + rows - 1, rows)}
-    down = {"row": lax.rem(row + 1, rows)}
-    left = {"col": lax.rem(col + cols - 1, cols)}
-    right = {"col": lax.rem(col + 1, cols)}
-
-    p_in = pltpu.make_async_copy(p_hbm, pv, in_sem.at[0])
-    a_in = pltpu.make_async_copy(a_hbm, av, in_sem.at[1])
-    p_in.start()
-    a_in.start()
+    has_up, has_down, has_left, has_right = row > 0, row < rows - 1, col > 0, col < cols - 1
+    up = ({"row": jnp.maximum(row - 1, 0)}, has_up, has_down)
+    down = ({"row": jnp.minimum(row + 1, rows - 1)}, has_down, has_up)
+    left = ({"col": jnp.maximum(col - 1, 0)}, has_left, has_right)
+    right = ({"col": jnp.minimum(col + 1, cols - 1)}, has_right, has_left)
+
     barrier = pltpu.get_barrier_semaphore()
-    for peer in (up, down, left, right):
-        pl.semaphore_signal(barrier, inc=1, device_id=peer, device_id_type=MESH)
-
-    def remote(number, src, dst, peer):
-        return pltpu.make_async_remote_copy(
-            src_ref=src,
-            dst_ref=dst,
-            send_sem=send_sem.at[number],
-            recv_sem=recv_sem.at[number],
-            device_id=peer,
-            device_id_type=MESH,
-        )
+    for peer, there, _ in (up, down, left, right):
+
+        @pl.when(there)
+        def _():
+            pl.semaphore_signal(barrier, inc=1, device_id=peer, device_id_type=MESH)
+
+    arrays = (
+        (p_hbm, pv), (a_hbm, av), (fine_columns_hbm, fine_columns), (fine_counts_hbm, fine_counts),
+        (prolong_columns_hbm, prolong_columns), (prolong_counts_hbm, prolong_counts),
+    )
+    p_in, a_in, *codes_in = [
+        pltpu.make_async_copy(src, dst, in_sem.at[at]) for at, (src, dst) in enumerate(arrays)
+    ]
+    for copy in (*codes_in, p_in, a_in):
+        copy.start()
+
+    class Remote:
+        def __init__(self, number, src, dst, side):
+            peer, self.sends, self.receives = side
+            self.copy = pltpu.make_async_remote_copy(
+                src_ref=src,
+                dst_ref=dst,
+                send_sem=send_sem.at[number],
+                recv_sem=recv_sem.at[number],
+                device_id=peer,
+                device_id_type=MESH,
+            )
+
+        def start(self):
+            pl.when(self.sends)(self.copy.start)
+
+        def wait_send(self):
+            pl.when(self.sends)(self.copy.wait_send)
+
+        def wait_recv(self):
+            pl.when(self.receives)(self.copy.wait_recv)
+
+    remote = Remote
+
+    for there, refs in (
+        (has_up, (halo_t, got_u)),
+        (has_down, (halo_b, got_d)),
+        (has_left, (halo_l, corner_l, got_l)),
+        (has_right, (halo_r, corner_r, got_r)),
+    ):
+
+        @pl.when(jnp.logical_not(there))
+        def _():
+            for ref in refs:
+                ref[...] = jnp.zeros(ref.shape, ref.dtype)
 
     eye = (
         lax.broadcasted_iota(jnp.int32, (256, 256), 0)
@@ -130,6 +166,8 @@
         code += lax.shift_right_logical(number, cols.bit_length() - 1)
         return jnp.where(p < prolong_counts[u, v], code, UNUSED)
 
+    for copy in codes_in:
+        copy.wait()
     codes = {(u, v): [home_code(u, v, p) for p in range(KP)] for u in range(AG) for v in range(AG)}
 
     def code_tile(ref, at, first, second):
@@ -152,7 +190,7 @@
             eye, pv[u].reshape(256, 256)
         ).astype(BF16)
 
-    pl.semaphore_wait(barrier, 4)
+    pl.semaphore_wait(barrier, sum(side[1].astype(jnp.int32) for side in (up, down, left, right)))
     to_up = remote(0, ptx.at[:, 0:256], halo_b, up)
     to_down = remote(1, ptx.at[:, 768:1024], halo_t, down)
     to_left = remote(2, edge_l, halo_r, left)
@@ -349,14 +387,17 @@
     fine_blocks, fine_columns, fine_counts, prolong_blocks, prolong_columns, prolong_counts
 ):
     vmem = pl.BlockSpec(memory_space=pltpu.VMEM)
-    smem = pl.BlockSpec(memory_space=pltpu.SMEM)
-    hbm = pl.BlockSpec(memory_space=pl.ANY)
+    hbm = pl.BlockSpec(memory_space=pltpu.HBM)
     return pl.pallas_call(
         kernel,
         out_shape=jax.ShapeDtypeStruct((1, 1, B, 49 * B), BF16),
-        in_specs=[hbm, hbm, smem, smem, smem, smem],
+        in_specs=[hbm] * 6,
         out_specs=vmem,
         scratch_shapes=[
+            pltpu.SMEM((AG, AG, KA), jnp.int32),
+            pltpu.SMEM((AG, AG), jnp.int32),
+            pltpu.SMEM((AG, AG, KP), jnp.int32),
+            pltpu.SMEM((AG, AG), jnp.int32),
             pltpu.VMEM((AG, AG, B, KP * B), BF16),
             pltpu.VMEM((AG, AG, B, KA * B), BF16),
             pltpu.VMEM((PT_ROWS, 1024), BF16),
@@ -388,12 +429,12 @@
             pltpu.VMEM((B, FULL), F32),
             pltpu.VMEM((B, FULL), BF16),
             pltpu.VMEM((B, FULL), BF16),
-            pltpu.SemaphoreType.DMA((2,)),
+            pltpu.SemaphoreType.DMA((6,)),
             pltpu.SemaphoreType.DMA((12,)),
             pltpu.SemaphoreType.DMA((12,)),
         ],
         compiler_params=pltpu.CompilerParams(
-            collective_id=0, has_side_effects=True, vmem_limit_bytes=60 * 2**20
+            collective_id=0, has_side_effects=True, vmem_limit_bytes=62 * 2**20
         ),
     )(
         prolong_blocks, fine_blocks,

time: 37.8 us -> 32.2 us (0.85)
  the two profiles are of different devices: /device:TPU:24 before, /device:TPU:105 now
where the time goes in v2:
time: 32.2 us; the launch traced here: 32.1 us
  Pallas kernels  30.3 us (94%)
  local copies, waits for them, and re-layouts  1.78 us (6%)
    pallas_call x1, Pallas kernels, per_device(): pl.pallas_call(kernel, out_shape=jax.ShapeDtypeStruct((1, 1, B, 49 * B),...  30.3 us
    unnamed x1, local copies, waits for them, and re-layouts  1.78 us

profile of v2, /device:TPU:105, one launch (start us, length us, event | category | flops | bytes accessed | tf_op | source)
XLA Modules:
  0.0 32.1 jit_solution(9518888920795445914)
XLA Ops:
  0.0 30.3 %shard_map.64 = bf16[1,1,64,3136]{3,2,1,0:T(8,128)(2,1)} custom-call(bf16[4,4,64,256]{3,2,1,0:T(8,128)(2,1)} %p_hbm.1, bf16[4,4,64,576]{3,2,1,0:T(8,128)(2,1)} %a_hbm.1, s32[4,4,9]{2,1,0:T(4,128)} %fine_columns_hbm.1, s32[4,4]{1,0:T(4,128)} %fine_counts_hbm.1, s32[4,4,4]{2,1,0:T(4,128)} %prolong_columns_hbm.1, s32[4,4]{1,0:T(4,128)} %prolong_counts_hbm.1), custom_call_target="tpu_custom_call" | custom-call | tf_op jit(solution)/shard_map/pallas_call | solution.py:391
  30.3 1.8 %copy.8 = bf16[1,1,64,3136]{3,2,1,0:T(8,128)(2,1)} copy(bf16[1,1,64,3136]{3,2,1,0:T(8,128)(2,1)} %shard_map.64) | data formatting | bytes 802816

commit v3 on v2

--- a/solution.py
+++ b/solution.py
@@ -20,6 +20,7 @@
 ORDER = {-1: 0, 1: 1, 0: 2}
 WIDE = 26 * B
 FULL = 36 * B
+CHUNKS = 4
 R_ROWS = 17 * B
 
 
@@ -86,7 +87,7 @@
     p_hbm, a_hbm, fine_columns_hbm, fine_counts_hbm, prolong_columns_hbm, prolong_counts_hbm, out_ref,
     fine_columns, fine_counts, prolong_columns, prolong_counts,
     pv, av, ptx, edge_l, edge_r, halo_t, halo_b, halo_l, halo_r,
-    pass_l, pass_r, corner_l, corner_r,
+    pack_tl, pack_tr, pack_bl, pack_br, land_tl, land_tr, land_bl, land_br, corner_l, corner_r,
     pdt, aw, q_own, q_l, q_r, r_own, r_l, r_r, c_side, c_mid,
     send_l, send_r, got_l, got_r, send_rows, e_mid, got_u, got_d,
     in_sem, send_sem, recv_sem,
@@ -94,16 +95,22 @@
     row, col = lax.axis_index("row"), lax.axis_index("col")
     rows, cols = lax.axis_size("row"), lax.axis_size("col")
     fine_cols = AG * cols
-    has_up, has_down, has_left, has_right = row > 0, row < rows - 1, col > 0, col < cols - 1
-    up = ({"row": jnp.maximum(row - 1, 0)}, has_up, has_down)
-    down = ({"row": jnp.minimum(row + 1, rows - 1)}, has_down, has_up)
-    left = ({"col": jnp.maximum(col - 1, 0)}, has_left, has_right)
-    right = ({"col": jnp.minimum(col + 1, cols - 1)}, has_right, has_left)
+    def there(d, s):
+        r, c = row + d, col + s
+        return jnp.logical_and(jnp.logical_and(r >= 0, r < rows), jnp.logical_and(c >= 0, c < cols))
+
+    def side(d, s):
+        peer = {"row": jnp.clip(row + d, 0, rows - 1), "col": jnp.clip(col + s, 0, cols - 1)}
+        return peer, there(d, s), there(-d, -s)
+
+    up, down, left, right = side(-1, 0), side(1, 0), side(0, -1), side(0, 1)
+    up_left, up_right, down_left, down_right = side(-1, -1), side(-1, 1), side(1, -1), side(1, 1)
+    sides = (up, down, left, right, up_left, up_right, down_left, down_right)
 
     barrier = pltpu.get_barrier_semaphore()
-    for peer, there, _ in (up, down, left, right):
-
-        @pl.when(there)
+    for peer, present, _ in sides:
+
+        @pl.when(present)
         def _():
             pl.semaphore_signal(barrier, inc=1, device_id=peer, device_id_type=MESH)
 
@@ -140,14 +147,18 @@
 
     remote = Remote
 
-    for there, refs in (
-        (has_up, (halo_t, got_u)),
-        (has_down, (halo_b, got_d)),
-        (has_left, (halo_l, corner_l, got_l)),
-        (has_right, (halo_r, corner_r, got_r)),
+    for (_, present, _), refs in (
+        (up, (halo_t, got_u)),
+        (down, (halo_b, got_d)),
+        (left, (halo_l, got_l)),
+        (right, (halo_r, got_r)),
+        (up_left, (land_tl,)),
+        (up_right, (land_tr,)),
+        (down_left, (land_bl,)),
+        (down_right, (land_br,)),
     ):
 
-        @pl.when(jnp.logical_not(there))
+        @pl.when(jnp.logical_not(present))
         def _():
             for ref in refs:
                 ref[...] = jnp.zeros(ref.shape, ref.dtype)
@@ -190,12 +201,37 @@
             eye, pv[u].reshape(256, 256)
         ).astype(BF16)
 
-    pl.semaphore_wait(barrier, sum(side[1].astype(jnp.int32) for side in (up, down, left, right)))
+    low, high, last = slice(0, 2 * B), slice(2 * B, 4 * B), slice(KP * B, PT_ROWS)
+    for pack, at, in_right, is_top in (
+        (pack_tl, 0, False, False),
+        (pack_tr, 1, True, False),
+        (pack_bl, 6, False, True),
+        (pack_br, 7, True, True),
+    ):
+        tile = slice(at * 128, (at + 1) * 128)
+        first, second = (low, high) if is_top else (high, low)
+        one, two = ptx[first, tile].astype(F32), ptx[second, tile].astype(F32)
+        if in_right:
+            one = pltpu.roll(one, B, 1)
+        else:
+            two = pltpu.roll(two, B, 1)
+        pack[0 : 2 * B, :] = jnp.where(half, one, two).astype(BF16)
+        code = ptx[last, tile].astype(F32)
+        pack[2 * B :, :] = (pltpu.roll(code, B, 1) if in_right == is_top else code).astype(BF16)
+
+    pl.semaphore_wait(barrier, sum(present.astype(jnp.int32) for _, present, _ in sides))
     to_up = remote(0, ptx.at[:, 0:256], halo_b, up)
     to_down = remote(1, ptx.at[:, 768:1024], halo_t, down)
     to_left = remote(2, edge_l, halo_r, left)
     to_right = remote(3, edge_r, halo_l, right)
-    for copy in (to_up, to_down, to_left, to_right):
+    corners_out = (
+        remote(4, pack_tl, land_br, up_left),
+        remote(5, pack_tr, land_bl, up_right),
+        remote(24, pack_bl, land_tr, down_left),
+        remote(25, pack_br, land_tl, down_right),
+    )
+    halo_out = (to_up, to_down, to_left, to_right, *corners_out)
+    for copy in halo_out:
         copy.start()
 
     def own_dense(u, carry):
@@ -282,19 +318,6 @@
 
     to_down.wait_recv()
     to_up.wait_recv()
-    for rows_16 in range(PT_ROWS // 16):
-        at = slice(rows_16 * 16, (rows_16 + 1) * 16)
-        pass_l[at, :] = jnp.where(
-            half, halo_t[at, 0:128].astype(F32), swapped(halo_b[at, 0:128])
-        ).astype(BF16)
-        pass_r[at, :] = jnp.where(
-            half, swapped(halo_t[at, 128:256]), halo_b[at, 128:256].astype(F32)
-        ).astype(BF16)
-    corner_to_left = remote(4, pass_l, corner_r, left)
-    corner_to_right = remote(5, pass_r, corner_l, right)
-    corner_to_left.start()
-    corner_to_right.start()
-
     for halo, shift, blanks, first in ((halo_t, 1, (3, 4), 1024), (halo_b, 3, (0, 1), 1280)):
         at = slice(first, first + 256)
         dense(
@@ -313,8 +336,13 @@
         )
     c_side[:, 256:1280] += dot_nt(q_own[0:384, 1024:1536], r_own[0:1024, 1024:1536])
 
-    corner_to_left.wait_recv()
-    corner_to_right.wait_recv()
+    for copy in corners_out:
+        copy.wait_recv()
+    for top, bottom, corner in ((land_tl, land_bl, corner_l), (land_tr, land_br, corner_r)):
+        one, two = top[0 : 2 * B, :], bottom[0 : 2 * B, :]
+        corner[low, :] = jnp.where(half, one, two)
+        corner[high, :] = swapped(jnp.where(half, two, one)).astype(BF16)
+        corner[last, :] = jnp.where(half, top[2 * B :, :], bottom[2 * B :, :])
     for corner, ref in ((corner_l, r_l), (corner_r, r_r)):
         spread, blocks = slot_parts(corner, slice(0, 128), 128)
         for side in (-1, 0, 1):
@@ -329,57 +357,82 @@
     c_side[:, 0:1024] += dot_nt(q_l[0:384, :], r_l[64:1088, :])
     c_side[:, 640:WIDE] += dot_nt(q_r[0:384, :], r_r[64:1088, :])
 
-    send_l[...] = c_side[0:192, :].astype(BF16)
-    send_r[...] = c_side[192:384, :].astype(BF16)
     side_copies = []
-    for number, at in ((6, slice(0, 128)), (8, slice(128, 192))):
-        to_l = remote(number, send_l.at[at], got_r.at[at], left)
-        to_r = remote(number + 1, send_r.at[at], got_l.at[at], right)
-        to_l.start()
-        to_r.start()
-        side_copies.append((to_l, to_r))
+    for q in range(CHUNKS):
+        for h in range(2):
+            at, first = slice(q * 32 + h * 16, q * 32 + h * 16 + 16), h * B + q * 16
+            send_l[at, :] = c_side[first : first + 16, :].astype(BF16)
+            send_r[at, :] = c_side[192 + first : 208 + first, :].astype(BF16)
+        at = slice(q * 32, q * 32 + 32)
+        pair = (
+            remote(6 + 2 * q, send_l.at[at], got_r.at[at], left),
+            remote(7 + 2 * q, send_r.at[at], got_l.at[at], right),
+        )
+        for copy in pair:
+            copy.start()
+        side_copies.append(pair)
+    send_l[128:192, :] = c_side[128:192, :].astype(BF16)
+    send_r[128:192, :] = c_side[320:384, :].astype(BF16)
 
     c_mid[:, 384:1408] += dot_nt(q_own[384:576, 1024:1536], r_own[64:1088, 1024:1536])
     c_mid[:, 0:1024] += dot_nt(q_l[384:576, :], r_l[0:1024, :])
     c_mid[:, 640:WIDE] += dot_nt(q_r[384:576, :], r_r[0:1024, :])
 
-    def folded(at, lo, hi):
+    def folded(got_at, mid_at, lo, hi):
         total = None
-        for ref, first in ((got_l, 0), (c_mid, 256), (got_r, 640)):
+        for ref, at, first in ((got_l, got_at, 0), (c_mid, mid_at, 256), (got_r, got_at, 640)):
             if first <= lo and hi <= first + WIDE:
                 part = ref[at, lo - first : hi - first].astype(F32)
                 total = part if total is None else total + part
         return total
 
     spans = ((0, 256), (256, 640), (640, 1664), (1664, 1920), (1920, FULL))
-    for copy in side_copies[0]:
+    row_copies = []
+    for q in range(CHUNKS):
+        for copy in side_copies[q]:
+            copy.wait_recv()
+        for h in range(2):
+            at, first = slice(q * 32 + h * 16, q * 32 + h * 16 + 16), h * B + q * 16
+            for lo, hi in spans:
+                send_rows[at, lo:hi] = folded(at, slice(first, first + 16), lo, hi).astype(BF16)
+        at = slice(q * 16, q * 16 + 16)
+        pair = (
+            remote(16 + 2 * q, send_rows.at[q * 32 : q * 32 + 16], got_d.at[at], up),
+            remote(17 + 2 * q, send_rows.at[q * 32 + 16 : q * 32 + 32], got_u.at[at], down),
+        )
+        for copy in pair:
+            copy.start()
+        row_copies.append(pair)
+    at = slice(128, 192)
+    side_copies.append(
+        (
+            remote(14, send_l.at[at], got_r.at[at], left),
+            remote(15, send_r.at[at], got_l.at[at], right),
+        )
+    )
+    for copy in side_copies[CHUNKS]:
+        copy.start()
+    for copy in side_copies[CHUNKS]:
         copy.wait_recv()
     for lo, hi in spans:
-        send_rows[:, lo:hi] = folded(slice(0, 128), lo, hi).astype(BF16)
-    to_u = remote(10, send_rows.at[0:64], got_d, up)
-    to_d = remote(11, send_rows.at[64:128], got_u, down)
-    to_u.start()
-    to_d.start()
-    for copy in side_copies[1]:
-        copy.wait_recv()
-    for lo, hi in spans:
-        e_mid[:, lo:hi] = folded(slice(128, 192), lo, hi)
-    to_u.wait_recv()
-    to_d.wait_recv()
-
-    for s in range(7):
-        for t in range(7):
-            total = None
-            for ref, j in ((got_u, s), (e_mid, s - 1), (got_d, s - 2)):
-                if 0 <= j < 5:
-                    at = (t * 5 + j) * B
-                    part = ref[:, at : at + B].astype(F32)
-                    total = part if total is None else total + part
-            at = (s * 7 + t) * B
-            out_ref[0, 0, :, at : at + B] = total.astype(BF16)
-
-    sent = [to_up, to_down, to_left, to_right, corner_to_left, corner_to_right, to_u, to_d]
-    for copy in sent + [copy for pair in side_copies for copy in pair]:
+        e_mid[:, lo:hi] = folded(at, at, lo, hi)
+
+    for q in range(CHUNKS):
+        for copy in row_copies[q]:
+            copy.wait_recv()
+        rows_16 = slice(q * 16, q * 16 + 16)
+        for s in range(7):
+            for t in range(7):
+                total = None
+                for ref, j in ((got_u, s), (e_mid, s - 1), (got_d, s - 2)):
+                    if 0 <= j < 5:
+                        at = (t * 5 + j) * B
+                        part = ref[rows_16, at : at + B].astype(F32)
+                        total = part if total is None else total + part
+                at = (s * 7 + t) * B
+                out_ref[0, 0, rows_16, at : at + B] = total.astype(BF16)
+
+    for copy in [*halo_out] + [copy for pair in side_copies + row_copies for copy in pair]:
         copy.wait_send()
 
 
@@ -407,8 +460,7 @@
             pltpu.VMEM((PT_ROWS, 256), BF16),
             pltpu.VMEM((PT_ROWS, 256), BF16),
             pltpu.VMEM((PT_ROWS, 256), BF16),
-            pltpu.VMEM((PT_ROWS, 128), BF16),
-            pltpu.VMEM((PT_ROWS, 128), BF16),
+            *[pltpu.VMEM((2 * B + 16, 128), BF16)] * 8,
             pltpu.VMEM((PT_ROWS, 128), BF16),
             pltpu.VMEM((PT_ROWS, 128), BF16),
             pltpu.VMEM((9 * B, 1024), BF16),
@@ -430,8 +482,8 @@
             pltpu.VMEM((B, FULL), BF16),
             pltpu.VMEM((B, FULL), BF16),
             pltpu.SemaphoreType.DMA((6,)),
-            pltpu.SemaphoreType.DMA((12,)),
-            pltpu.SemaphoreType.DMA((12,)),
+            pltpu.SemaphoreType.DMA((26,)),
+            pltpu.SemaphoreType.DMA((26,)),
         ],
         compiler_params=pltpu.CompilerParams(
             collective_id=0, has_side_effects=True, vmem_limit_bytes=62 * 2**20

time: 32.2 us -> 28 us (0.87); the launches traced: 32.1 us -> 27.5 us
  Pallas kernels: 30.3 us -> 25.7 us
    pallas_call x1, Pallas kernels: 30.3 us -> 25.7 us  [per_device(): pl.pallas_call(kernel, out_shape=jax.ShapeDtypeStruct((1, 1, B, 49 * B),...]
where the time goes in v3:
time: 28 us; the launch traced here: 27.5 us
  Pallas kernels  25.7 us (92%)
  local copies, waits for them, and re-layouts  1.78 us (6%)
    pallas_call x1, Pallas kernels, per_device(): pl.pallas_call(kernel, out_shape=jax.ShapeDtypeStruct((1, 1, B, 49 * B),...  25.7 us
    unnamed x1, local copies, waits for them, and re-layouts  1.78 us

profile of v3, /device:TPU:105, one launch (start us, length us, event | category | flops | bytes accessed | tf_op | source)
XLA Modules:
  0.0 27.5 jit_solution(14449852226743996655)
XLA Ops:
  0.0 25.7 %shard_map.64 = bf16[1,1,64,3136]{3,2,1,0:T(8,128)(2,1)} custom-call(bf16[4,4,64,256]{3,2,1,0:T(8,128)(2,1)} %p_hbm.1, bf16[4,4,64,576]{3,2,1,0:T(8,128)(2,1)} %a_hbm.1, s32[4,4,9]{2,1,0:T(4,128)} %fine_columns_hbm.1, s32[4,4]{1,0:T(4,128)} %fine_counts_hbm.1, s32[4,4,4]{2,1,0:T(4,128)} %prolong_columns_hbm.1, s32[4,4]{1,0:T(4,128)} %prolong_counts_hbm.1), custom_call_target="tpu_custom_call" | custom-call | tf_op jit(solution)/shard_map/pallas_call | solution.py:444
  25.7 1.8 %copy.8 = bf16[1,1,64,3136]{3,2,1,0:T(8,128)(2,1)} copy(bf16[1,1,64,3136]{3,2,1,0:T(8,128)(2,1)} %shard_map.64) | data formatting | bytes 802816

commit v4 on v3

--- a/solution.py
+++ b/solution.py
@@ -21,6 +21,7 @@
 WIDE = 26 * B
 FULL = 36 * B
 CHUNKS = 4
+PLACES = (0, 3, 1, 2)
 R_ROWS = 17 * B
 
 
@@ -87,8 +88,8 @@
     p_hbm, a_hbm, fine_columns_hbm, fine_counts_hbm, prolong_columns_hbm, prolong_counts_hbm, out_ref,
     fine_columns, fine_counts, prolong_columns, prolong_counts,
     pv, av, ptx, edge_l, edge_r, halo_t, halo_b, halo_l, halo_r,
-    pack_tl, pack_tr, pack_bl, pack_br, land_tl, land_tr, land_bl, land_br, corner_l, corner_r,
-    pdt, aw, q_own, q_l, q_r, r_own, r_l, r_r, c_side, c_mid,
+    pass_l, pass_r, corner_l, corner_r,
+    pdt, pdt_l, pdt_r, aw, aw_l, aw_r, q_own, q_l, q_r, r_own, r_l, r_r, c_side, c_mid,
     send_l, send_r, got_l, got_r, send_rows, e_mid, got_u, got_d,
     in_sem, send_sem, recv_sem,
 ):
@@ -104,8 +105,7 @@
         return peer, there(d, s), there(-d, -s)
 
     up, down, left, right = side(-1, 0), side(1, 0), side(0, -1), side(0, 1)
-    up_left, up_right, down_left, down_right = side(-1, -1), side(-1, 1), side(1, -1), side(1, 1)
-    sides = (up, down, left, right, up_left, up_right, down_left, down_right)
+    sides = (up, down, left, right)
 
     barrier = pltpu.get_barrier_semaphore()
     for peer, present, _ in sides:
@@ -150,12 +150,8 @@
     for (_, present, _), refs in (
         (up, (halo_t, got_u)),
         (down, (halo_b, got_d)),
-        (left, (halo_l, got_l)),
-        (right, (halo_r, got_r)),
-        (up_left, (land_tl,)),
-        (up_right, (land_tr,)),
-        (down_left, (land_bl,)),
-        (down_right, (land_br,)),
+        (left, (halo_l, corner_l, got_l)),
+        (right, (halo_r, corner_r, got_r)),
     ):
 
         @pl.when(jnp.logical_not(present))
@@ -188,8 +184,8 @@
         ref[KP * B :, at * 128 : (at + 1) * 128] = tile.astype(F32).astype(BF16)
 
     for u in range(AG):
-        code_tile(ptx, 2 * u, (u, 0), (u, 1))
-        code_tile(ptx, 2 * u + 1, (u, 2), (u, 3))
+        code_tile(ptx, 2 * u, (u, 0), (u, 3))
+        code_tile(ptx, 2 * u + 1, (u, 1), (u, 2))
     for side, edge in ((0, edge_l), (AG - 1, edge_r)):
         code_tile(edge, 0, (0, side), (1, side))
         code_tile(edge, 1, (2, side), (3, side))
@@ -198,40 +194,18 @@
         edge[0 : KP * B, :] = dot_nt(eye, pv[:, side].reshape(256, 256)).astype(BF16)
     for u in range(AG):
         ptx[0 : KP * B, u * 256 : (u + 1) * 256] = dot_nt(
-            eye, pv[u].reshape(256, 256)
+            eye, jnp.concatenate([pv[u, v] for v in PLACES], axis=0)
         ).astype(BF16)
 
-    low, high, last = slice(0, 2 * B), slice(2 * B, 4 * B), slice(KP * B, PT_ROWS)
-    for pack, at, in_right, is_top in (
-        (pack_tl, 0, False, False),
-        (pack_tr, 1, True, False),
-        (pack_bl, 6, False, True),
-        (pack_br, 7, True, True),
-    ):
-        tile = slice(at * 128, (at + 1) * 128)
-        first, second = (low, high) if is_top else (high, low)
-        one, two = ptx[first, tile].astype(F32), ptx[second, tile].astype(F32)
-        if in_right:
-            one = pltpu.roll(one, B, 1)
-        else:
-            two = pltpu.roll(two, B, 1)
-        pack[0 : 2 * B, :] = jnp.where(half, one, two).astype(BF16)
-        code = ptx[last, tile].astype(F32)
-        pack[2 * B :, :] = (pltpu.roll(code, B, 1) if in_right == is_top else code).astype(BF16)
-
     pl.semaphore_wait(barrier, sum(present.astype(jnp.int32) for _, present, _ in sides))
-    to_up = remote(0, ptx.at[:, 0:256], halo_b, up)
-    to_down = remote(1, ptx.at[:, 768:1024], halo_t, down)
-    to_left = remote(2, edge_l, halo_r, left)
-    to_right = remote(3, edge_r, halo_l, right)
-    corners_out = (
-        remote(4, pack_tl, land_br, up_left),
-        remote(5, pack_tr, land_bl, up_right),
-        remote(24, pack_bl, land_tr, down_left),
-        remote(25, pack_br, land_tl, down_right),
-    )
-    halo_out = (to_up, to_down, to_left, to_right, *corners_out)
-    for copy in halo_out:
+    to_left = remote(0, edge_l, halo_r, left)
+    to_right = remote(1, edge_r, halo_l, right)
+    ends, inner = slice(0, 128), slice(128, 256)
+    ends_up = remote(2, ptx.at[:, 0:128], halo_b.at[:, ends], up)
+    ends_down = remote(3, ptx.at[:, 768:896], halo_t.at[:, ends], down)
+    inner_up = remote(4, ptx.at[:, 128:256], halo_b.at[:, inner], up)
+    inner_down = remote(5, ptx.at[:, 896:1024], halo_t.at[:, inner], down)
+    for copy in (ends_up, ends_down, inner_up, inner_down, to_left, to_right):
         copy.start()
 
     def own_dense(u, carry):
@@ -247,9 +221,12 @@
         return carry
 
     lax.fori_loop(0, AG, own_dense, 0)
+    for edge, ref in ((edge_l, pdt_l), (edge_r, pdt_r)):
+        lanes = slice(0, 256)
+        dense(edge, lanes, 256, lambda d, s: [(ref, term_row(d, s), lanes)], [])
 
     a_in.wait()
-    tiles = ((1, 2), (3, 4), (0, 5))
+    tiles = ((1, 4), (2, 3))
 
     def toward_code(u, v, k):
         number = fine_columns[u, v, k]
@@ -270,54 +247,109 @@
                 one, two = toward[2 * t], toward[2 * t + 1]
                 codes = jnp.where(line == t, jnp.where(half, one, two), codes)
                 codes = jnp.where(line == t + 5, jnp.where(half, two, one), codes)
-            for at, pair in enumerate(tiles):
-                sides = [target - 1 - v for target in pair]
-                for dr in (-1, 0, 1):
-                    here = (u + dr + 1, pl.ds((1 - dr) * 256 + v * B, B), pl.ds(at * 128, 128))
-                    wanted = [(dr + 1) * 3 + dc + 1 if abs(dc) <= 1 else 99 for dc in sides]
-                    if wanted == [99, 99]:
-                        aw[here] = jnp.zeros((B, 128), BF16)
-                        continue
-                    match = jnp.where(
-                        codes == jnp.where(half, wanted[0], wanted[1]), 1.0, 0.0
-                    )
-                    total = None
-                    for t in range(10):
-                        if wanted[0] == 99 and t == 4 or wanted[1] == 99 and t == 9:
-                            continue
+            def gathered(wanted, skip=()):
+                match = jnp.where(codes == jnp.where(half, wanted[0], wanted[1]), 1.0, 0.0)
+                total = None
+                for t in range(10):
+                    if t not in skip:
                         mask = jnp.broadcast_to(match[t : t + 1], (16, 128)).astype(BF16)
                         part = mask[None] * wide[t]
                         total = part if total is None else total + part
-                    aw[here] = total.reshape(B, 128)
+                return total.reshape(B, 128)
+
+            for at, pair in enumerate(tiles):
+                steps = [target - 1 - v for target in pair]
+                for dr in (-1, 0, 1):
+                    here = (u + dr + 1, pl.ds((1 - dr) * 256 + PLACES.index(v) * B, B), pl.ds(at * 128, 128))
+                    wanted = [(dr + 1) * 3 + dc + 1 if abs(dc) <= 1 else 99 for dc in steps]
+                    if wanted == [99, 99]:
+                        aw[here] = jnp.zeros((B, 128), BF16)
+                    else:
+                        aw[here] = gathered(wanted)
+            if v in (0, AG - 1):
+                ref, dc = (aw_l, -1) if v == 0 else (aw_r, 1)
+                for at, pair in enumerate(((0, 1), (2, 3), (-1, 4))):
+                    steps = [target - u for target in pair]
+                    wanted = [jnp.where(jnp.abs(dr) <= 1, (dr + 1) * 3 + dc + 1, 99) for dr in steps]
+                    ref[pl.ds(u * B, B), at * 128 : (at + 1) * 128] = gathered(wanted)
         return carry
 
     lax.fori_loop(0, AG, strip, 0)
 
-    def row_of_targets(w):
-        first, last = max(w - 1, 0), min(w + 1, AG - 1)
-        got = dot_nn(
-            pdt[:, first * 256 : (last + 1) * 256],
-            aw[w + 1, (first - w + 1) * 256 : (last - w + 2) * 256, :],
+    for w in range(-1, AG + 1):
+        low_u, high_u = max(w - 1, 0), min(w + 1, AG - 1)
+        place = w if 0 <= w < AG else (AG if w < 0 else AG + 1)
+        q_own[:, place * 256 : (place + 1) * 256] = dot_nn(
+            pdt[:, low_u * 256 : (high_u + 1) * 256],
+            aw[w + 1, (low_u - w + 1) * 256 : (high_u - w + 2) * 256, :],
+        ).astype(BF16)
+    q_l[...] = dot_nn(pdt_l[...], aw_l[...]).astype(BF16)
+    q_r[...] = dot_nn(pdt_r[...], aw_r[...]).astype(BF16)
+
+    def joined(ref, first, second, keep):
+        for at in range(0, PT_ROWS, 16):
+            one, two = first[at : at + 16, :].astype(F32), second[at : at + 16, :].astype(F32)
+            one = one if keep[0] else pltpu.roll(one, B, 1)
+            two = two if keep[1] else pltpu.roll(two, B, 1)
+            ref[at : at + 16, :] = jnp.where(half, one, two).astype(BF16)
+
+    ends_up.wait_recv()
+    ends_down.wait_recv()
+    joined(pass_l, halo_t.at[:, ends], halo_b.at[:, ends], (True, False))
+    joined(pass_r, halo_t.at[:, ends], halo_b.at[:, ends], (False, True))
+    corner_to_left = remote(24, pass_l, corner_r, left)
+    corner_to_right = remote(25, pass_r, corner_l, right)
+    corner_to_left.start()
+    corner_to_right.start()
+    halo_out = (
+        ends_up, ends_down, inner_up, inner_down, to_left, to_right,
+        corner_to_left, corner_to_right,
+    )
+
+    def add_terms(kind, q_ref, q_lanes, r_ref, r_lanes, base, first, fresh=False):
+        ref, at, shift = (c_side, slice(0, 384), 0) if kind == "side" else (c_mid, slice(384, 576), B)
+        for j in range(3):
+            lane_at = base + shift + (j * 5 + first) * B
+            row_at = window_row(first, j)
+            if lane_at % 128:
+                lane_at, row_at = lane_at - B, row_at - B
+            part = dot_nt(q_ref[at, q_lanes], r_ref[row_at : row_at + 256, r_lanes])
+            window = slice(lane_at, lane_at + 256)
+            ref[:, window] = part if fresh else ref[:, window] + part
+
+    def corner_terms(kind):
+        corners = slice(256, 384)
+        if kind == "side":
+            c_side[:, 0:1024] += dot_nt(q_l[0:384, corners], r_l[64:1088, corners])
+            c_side[:, 640:WIDE] += dot_nt(q_r[0:384, corners], r_r[64:1088, corners])
+        else:
+            c_mid[:, 0:1024] += dot_nt(q_l[384:576, corners], r_l[0:1024, corners])
+            c_mid[:, 640:WIDE] += dot_nt(q_r[384:576, corners], r_r[0:1024, corners])
+
+    own, over, under = slice(0, 1024), slice(1024, 1280), slice(1280, 1536)
+    nearby = slice(0, 256)
+    for ref, spans in (
+        (c_side, ((0, 384), (896, 1024), (1280, WIDE))),
+        (c_mid, ((0, 384), (640, 768), (1280, WIDE))),
+    ):
+        for lo, hi in spans:
+            ref[:, lo:hi] = jnp.zeros((ref.shape[0], hi - lo), F32)
+    add_terms("side", q_own, own, r_own, own, 5 * B, 1, True)
+
+    to_left.wait_recv()
+    to_right.wait_recv()
+    for halo, ref in ((halo_l, r_l), (halo_r, r_r)):
+        lanes = slice(0, 256)
+        dense(
+            halo, lanes, 256,
+            lambda d, s: [(ref, window_row(d + 2, s + 1), lanes)],
+            blank_rows(ref, lanes, (0, 4)),
         )
-        place = w if 0 <= w < AG else (AG if w < 0 else AG + 1)
-        q_own[:, place * 256 : (place + 1) * 256] = got[:, 0:256].astype(BF16)
-        return got[:, 256:384]
-
-    for at, (w0, w1) in enumerate(((0, 1), (2, 3), (-1, 4))):
-        x, y = row_of_targets(w0), row_of_targets(w1)
-        lanes = slice(at * 128, (at + 1) * 128)
-        q_l[:, lanes] = jnp.where(half, x, pltpu.roll(y, B, 1)).astype(BF16)
-        q_r[:, lanes] = jnp.where(half, pltpu.roll(x, B, 1), y).astype(BF16)
-
-    c_side[:, 0:256] = jnp.zeros((384, 256), F32)
-    c_side[:, 1280:WIDE] = jnp.zeros((384, WIDE - 1280), F32)
-    c_mid[:, 0:384] = jnp.zeros((192, 384), F32)
-    c_mid[:, 1408:WIDE] = jnp.zeros((192, WIDE - 1408), F32)
-    c_side[:, 256:1280] = dot_nt(q_own[0:384, 0:1024], r_own[0:1024, 0:1024])
-    c_mid[:, 384:1408] = dot_nt(q_own[384:576, 0:1024], r_own[64:1088, 0:1024])
-
-    to_down.wait_recv()
-    to_up.wait_recv()
+    add_terms("side", q_l, nearby, r_l, nearby, 0, 1)
+    add_terms("side", q_r, nearby, r_r, nearby, 10 * B, 1)
+
+    inner_up.wait_recv()
+    inner_down.wait_recv()
     for halo, shift, blanks, first in ((halo_t, 1, (3, 4), 1024), (halo_b, 3, (0, 1), 1280)):
         at = slice(first, first + 256)
         dense(
@@ -325,24 +357,11 @@
             lambda d, s: [(r_own, window_row(d + shift, s + 1), at)],
             blank_rows(r_own, at, blanks),
         )
-    to_left.wait_recv()
-    to_right.wait_recv()
-    for halo, ref in ((halo_l, r_l), (halo_r, r_r)):
-        at = slice(0, 256)
-        dense(
-            halo, at, 256,
-            lambda d, s: [(ref, window_row(d + 2, s + 1), at)],
-            blank_rows(ref, at, (0, 4)),
-        )
-    c_side[:, 256:1280] += dot_nt(q_own[0:384, 1024:1536], r_own[0:1024, 1024:1536])
-
-    for copy in corners_out:
-        copy.wait_recv()
-    for top, bottom, corner in ((land_tl, land_bl, corner_l), (land_tr, land_br, corner_r)):
-        one, two = top[0 : 2 * B, :], bottom[0 : 2 * B, :]
-        corner[low, :] = jnp.where(half, one, two)
-        corner[high, :] = swapped(jnp.where(half, two, one)).astype(BF16)
-        corner[last, :] = jnp.where(half, top[2 * B :, :], bottom[2 * B :, :])
+    add_terms("side", q_own, over, r_own, over, 5 * B, 0)
+    add_terms("side", q_own, under, r_own, under, 5 * B, 2)
+
+    corner_to_left.wait_recv()
+    corner_to_right.wait_recv()
     for corner, ref in ((corner_l, r_l), (corner_r, r_r)):
         spread, blocks = slot_parts(corner, slice(0, 128), 128)
         for side in (-1, 0, 1):
@@ -354,8 +373,7 @@
                 ref[row_at : row_at + B, 256:384] = chosen(spread, blocks, range(KP), code)
         for row_at in (0, 16 * B):
             ref[row_at : row_at + B, 256:384] = jnp.zeros((B, 128), BF16)
-    c_side[:, 0:1024] += dot_nt(q_l[0:384, :], r_l[64:1088, :])
-    c_side[:, 640:WIDE] += dot_nt(q_r[0:384, :], r_r[64:1088, :])
+    corner_terms("side")
 
     side_copies = []
     for q in range(CHUNKS):
@@ -374,9 +392,12 @@
     send_l[128:192, :] = c_side[128:192, :].astype(BF16)
     send_r[128:192, :] = c_side[320:384, :].astype(BF16)
 
-    c_mid[:, 384:1408] += dot_nt(q_own[384:576, 1024:1536], r_own[64:1088, 1024:1536])
-    c_mid[:, 0:1024] += dot_nt(q_l[384:576, :], r_l[0:1024, :])
-    c_mid[:, 640:WIDE] += dot_nt(q_r[384:576, :], r_r[0:1024, :])
+    add_terms("mid", q_own, own, r_own, own, 5 * B, 1, True)
+    add_terms("mid", q_l, nearby, r_l, nearby, 0, 1)
+    add_terms("mid", q_r, nearby, r_r, nearby, 10 * B, 1)
+    add_terms("mid", q_own, over, r_own, over, 5 * B, 0)
+    add_terms("mid", q_own, under, r_own, under, 5 * B, 2)
+    corner_terms("mid")
 
     def folded(got_at, mid_at, lo, hi):
         total = None
@@ -460,11 +481,13 @@
             pltpu.VMEM((PT_ROWS, 256), BF16),
             pltpu.VMEM((PT_ROWS, 256), BF16),
             pltpu.VMEM((PT_ROWS, 256), BF16),
-            *[pltpu.VMEM((2 * B + 16, 128), BF16)] * 8,
-            pltpu.VMEM((PT_ROWS, 128), BF16),
-            pltpu.VMEM((PT_ROWS, 128), BF16),
+            *[pltpu.VMEM((PT_ROWS, 128), BF16)] * 4,
             pltpu.VMEM((9 * B, 1024), BF16),
-            pltpu.VMEM((6, 768, 384), BF16),
+            pltpu.VMEM((9 * B, 256), BF16),
+            pltpu.VMEM((9 * B, 256), BF16),
+            pltpu.VMEM((6, 768, 256), BF16),
+            pltpu.VMEM((256, 384), BF16),
+            pltpu.VMEM((256, 384), BF16),
             pltpu.VMEM((9 * B, 1536), BF16),
             pltpu.VMEM((9 * B, 384), BF16),
             pltpu.VMEM((9 * B, 384), BF16),

time: 28 us -> 27.4 us (0.979)
  Pallas kernels: 25.7 us -> 25.4 us
    pallas_call x1, Pallas kernels: 25.7 us -> 25.4 us  [per_device(): pl.pallas_call(kernel, out_shape=jax.ShapeDtypeStruct((1, 1, B, 49 * B),...]
where the time goes in v4:
time: 27.4 us; the launch traced here: 27.2 us
  Pallas kernels  25.4 us (93%)
  local copies, waits for them, and re-layouts  1.78 us (6%)
    pallas_call x1, Pallas kernels, per_device(): pl.pallas_call(kernel, out_shape=jax.ShapeDtypeStruct((1, 1, B, 49 * B),...  25.4 us
    unnamed x1, local copies, waits for them, and re-layouts  1.78 us

profile of v4, /device:TPU:105, one launch (start us, length us, event | category | flops | bytes accessed | tf_op | source)
XLA Modules:
  0.0 27.2 jit_solution(805909795624320198)
XLA Ops:
  0.0 25.4 %shard_map.64 = bf16[1,1,64,3136]{3,2,1,0:T(8,128)(2,1)} custom-call(bf16[4,4,64,256]{3,2,1,0:T(8,128)(2,1)} %p_hbm.1, bf16[4,4,64,576]{3,2,1,0:T(8,128)(2,1)} %a_hbm.1, s32[4,4,9]{2,1,0:T(4,128)} %fine_columns_hbm.1, s32[4,4]{1,0:T(4,128)} %fine_counts_hbm.1, s32[4,4,4]{2,1,0:T(4,128)} %prolong_columns_hbm.1, s32[4,4]{1,0:T(4,128)} %prolong_counts_hbm.1), custom_call_target="tpu_custom_call" | custom-call | tf_op jit(solution)/shard_map/pallas_call | solution.py:465
  25.4 1.8 %copy.8 = bf16[1,1,64,3136]{3,2,1,0:T(8,128)(2,1)} copy(bf16[1,1,64,3136]{3,2,1,0:T(8,128)(2,1)} %shard_map.64) | data formatting | bytes 802816
